TPU v7x, 128 devices: a whole 4x4x4 slice. The times are simulated.
128 devices in a mesh: row: 4 (over x), col: 32 (over y, z, core).
Axes of the slice: x: 4, y: 4, z: 4, core: 2. Of those that a mesh axis runs over, the one named last changes fastest.
Arguments:
- features: bfloat16 [262144, 128], P(('row', 'col')), may hold values from -6 to 6
- self_one: bfloat16 [128, 256], replicated, may hold values from -0.5 to 0.5
- neigh_one: bfloat16 [128, 256], replicated, may hold values from -0.5 to 0.5
- self_two: bfloat16 [256, 172], replicated, may hold values from -0.375 to 0.375
- neigh_two: bfloat16 [256, 172], replicated, may hold values from -0.375 to 0.375
- tile_values: bfloat16 [24576, 128, 128], P(('row', 'col')), may hold values from 0 to 0.059814453
- tile_rows: int32 [128, 192], P(('row', 'col')), may hold values from 0 to 15, as said below
- tile_cols: int32 [128, 192], P(('row', 'col')), may hold values from 0 to 31
- tile_count: int32 [128], P(('row', 'col')), may hold values from 1 to 192, as said below
- part_size: int32 [128], P(('row', 'col')), may hold values from 256 to 2048, as said below
- send_rows: int32 [128, 128, 16], P(('row', 'col')), may hold values from 0 to 2047, as said below
- send_count: int32 [128, 128], replicated, may hold values from 0 to 16, as said below
- labels: int32 [262144], P(('row', 'col')), may hold values from 0 to 171
- train_mask: int32 [262144], P(('row', 'col')), may hold values 0 or 1
- stale_hidden: bfloat16 [262144, 256], P(('row', 'col')), may hold values from -6 to 6
- stale_grads: bfloat16 [262144, 256], P(('row', 'col')), may hold values from -0.059814453 to 0.059814453
Outputs:
- grad_self_one: float32 [128, 256], replicated
- grad_neigh_one: float32 [128, 256], replicated
- grad_self_two: float32 [256, 172], replicated
- grad_neigh_two: float32 [256, 172], replicated
- fresh_hidden: bfloat16 [262144, 256], P(('row', 'col'))
- fresh_grads: bfloat16 [262144, 256], P(('row', 'col'))
Inputs may be any that keep to these rules, and one draw needn't show every extreme that they name: `part_size`: one part holds exactly 2048 live nodes. `tile_count`: the largest part uses all 192 tile slots. `tile_rows`: tiles lie in row blocks that hold live nodes. `send_rows`: every entry is below the sending part's size. `send_count`: A part sends nothing to itself; some part receives 16 rows from every other part.
All inputs are finite; a program needn't handle non-finite values. No bound on the sum of `train_mask` on one device may be relied on, other than what follows from the above.
Results may differ from a plain program's by a relative error of at most 0.0095.
Values may be sent and summed in bfloat16 or wider, within the bound.
A program may use at most 128 MiB of HBM per device.

v0:
```python
import functools

import jax
import jax.numpy as jnp
from jax import lax
from jax.experimental import pallas as pl
from jax.experimental.pallas import tpu as pltpu
from jax.sharding import PartitionSpec as P

MESH = pl.DeviceIdType.MESH
F32 = jnp.float32
BF16 = jnp.bfloat16
NODE = 2048
HALO = 2048
BLK = 128
SLOT = 16
PARTS = 128
ROWS = 4
COLS = 32
TILES = 192
F_IN = 128
HID = 256
CLS = 172
CLSP = 176
CH = 512
NCH = 4
PIECES = 76
LOSS_SCALE = 1.0 / 32.0


def dot(a, b):
    return lax.dot_general(a, b, (((1,), (0,)), ((), ())), preferred_element_type=F32)


def dot_nt(a, b):
    return lax.dot_general(a, b, (((1,), (1,)), ((), ())), preferred_element_type=F32)


def at(start, size, mult=None):
    return pl.ds(pl.multiple_of(start, mult or size), size)


def device(index):
    return (index // COLS, lax.rem(index, COLS))


def owner_of(piece):
    return jnp.where(piece < 64, 2 * piece, 10 * (piece - 64) + 1)


def kernel(
    nxt, first, size_ref,
    feat_hbm, tiles_hbm, stale_hbm, grads_hbm,
    w1s_ref, w1n_ref, w2s_ref, w2n_ref, rows_ref, count_ref, labels_ref, mask_ref,
    gs1_ref, gn1_ref, gs2_ref, gn2_ref, fh_hbm, fg_hbm,
    adj, pick, chain, tbuf, own, both, halo, hidden, stale, grad_t, acc1, acc2, agg2,
    gl_t, ga_t, gp_t, recv_mask, send1, send2, send3, w2, contrib, part_in, result, small,
    tile_sem, load_sem, ssem, rsem, local_sem,
):
    my_row = lax.axis_index("row")
    my_col = lax.axis_index("col")
    me = my_row * COLS + my_col
    size = size_ref[0]

    barrier = pltpu.get_barrier_semaphore()

    def greet(i, c):
        pl.semaphore_signal(
            barrier, inc=1, device_id=device(jnp.bitwise_xor(me, i)), device_id_type=MESH
        )
        return c

    lax.fori_loop(1, PARTS, greet, 0)

    def load_tiles(k):
        return pltpu.make_async_copy(
            tiles_hbm.at[pl.ds(k * 48, 48)], tbuf.at[k % 2], tile_sem.at[k % 2]
        )

    load_own = pltpu.make_async_copy(feat_hbm, own, load_sem.at[0])
    load_own.start()
    load_tiles(3).start()
    load_tiles(2).start()
    load_stale = pltpu.make_async_copy(stale_hbm, stale, load_sem.at[1])
    load_stale.start()
    load_grads = pltpu.make_async_copy(grads_hbm, hidden, load_sem.at[2])
    load_grads.start()

    w2[...] = jnp.zeros_like(w2)
    w2[0:HID, 0:CLS] = w2s_ref[...]
    w2[HID : 2 * HID, 0:CLS] = w2n_ref[...]

    lanes128 = lax.broadcasted_iota(jnp.int32, (PARTS, BLK), 0)
    is_me = jnp.where(lanes128 == me, 1.0, 0.0).astype(BF16)
    counts = count_ref[...].astype(F32)
    in_count = dot(counts.astype(BF16), is_me).astype(BF16)
    out_count = dot(jnp.transpose(counts).astype(BF16), is_me).astype(BF16)
    rows = rows_ref[...]
    high = (rows // 128).astype(F32).astype(BF16)
    low = (rows % 128).astype(F32).astype(BF16)
    spread_ones = jnp.ones((SLOT, BLK), BF16)

    def build_pick(k, c):
        h = lax.broadcasted_iota(jnp.int32, (CH, PARTS), 0) + k * CH
        q = lax.broadcasted_iota(jnp.int32, (CH, PARTS), 1)
        expand = jnp.where(h // SLOT == q, 1.0, 0.0).astype(BF16)
        hs = lax.broadcasted_iota(jnp.int32, (CH, SLOT), 0)
        js = lax.broadcasted_iota(jnp.int32, (CH, SLOT), 1)
        slot_is = hs % SLOT == js
        high_b = dot(jnp.where(slot_is, dot(expand, high), 0.0).astype(BF16), spread_ones)
        low_b = dot(jnp.where(slot_is, dot(expand, low), 0.0).astype(BF16), spread_ones)
        j_of = (h % SLOT).astype(F32)
        live = j_of < dot(expand, out_count)
        recv_mask[at(k * CH, CH), :] = jnp.where(j_of < dot(expand, in_count), 1.0, 0.0)
        key = jnp.where(live & (low_b == q.astype(F32)), high_b, -1.0)
        for b in range(NODE // BLK):
            pick[at(k * CH, CH), b * BLK : (b + 1) * BLK] = jnp.where(
                key == float(b), 1.0, 0.0
            ).astype(BF16)
        return c

    lax.fori_loop(0, NCH, build_pick, 0)

    load_own.wait()

    def mask_own(k, c):
        row = lax.broadcasted_iota(jnp.int32, (CH, F_IN), 0) + k * CH
        kept = jnp.where(row < size, own[at(k * CH, CH), :].astype(F32), 0.0).astype(BF16)
        own[at(k * CH, CH), :] = kept
        both[at(k * CH, CH), 0:F_IN] = kept
        return c

    lax.fori_loop(0, NCH, mask_own, 0)

    def gather_feats(k, c):
        send1[at(k * CH, CH), :] = dot(pick[at(k * CH, CH), :], own[...]).astype(BF16)
        return c

    lax.fori_loop(0, NCH, gather_feats, 0)

    pl.semaphore_wait(barrier, PARTS - 1)

    def piece_of(index):
        return at(index * SLOT, SLOT)

    def send_to(src, dst, which, d):
        pltpu.make_async_remote_copy(
            src_ref=src.at[piece_of(d)],
            dst_ref=dst.at[piece_of(me)],
            send_sem=ssem.at[which],
            recv_sem=rsem.at[which],
            device_id=device(d),
            device_id_type=MESH,
        ).start()

    def send_feats(i, c):
        send_to(send1, halo, 0, jnp.bitwise_xor(me, i))
        return c

    lax.fori_loop(1, PARTS, send_feats, 0)
    halo[piece_of(me), :] = jnp.zeros((SLOT, F_IN), BF16)

    load_grads.wait()

    def turn_grads(k, c):
        grad_t[:, at(k * CH, CH)] = jnp.transpose(hidden[at(k * CH, CH), :])
        return c

    lax.fori_loop(0, NCH, turn_grads, 0)

    chain[TILES] = jnp.zeros((BLK, BLK), F32)
    for k in (3, 2, 1, 0):
        load_tiles(k).wait()

        def link(i, c, k=k):
            t = 47 - i
            chain[k * 48 + t] = tbuf[k % 2, t].astype(F32) + chain[nxt[k * 48 + t]]
            return c

        lax.fori_loop(0, 48, link, 0)
        if k >= 2:
            load_tiles(k - 2).start()

    def fill(r, c):
        for col in range(32):
            adj[at(r * BLK, BLK), col * BLK : (col + 1) * BLK] = chain[
                first[r * 32 + col]
            ].astype(BF16)
        return c

    lax.fori_loop(0, NODE // BLK, fill, 0)

    load_stale.wait()

    def mask_stale(k, c):
        live = recv_mask[at(k * CH, CH), :] > 0.0
        for half in range(2):
            cut = slice(half * BLK, (half + 1) * BLK)
            stale[at(k * CH, CH), cut] = jnp.where(
                live, stale[at(k * CH, CH), cut].astype(F32), 0.0
            ).astype(BF16)
        return c

    lax.fori_loop(0, NCH, mask_stale, 0)

    def early(k, c):
        cut = at(k * CH, CH)
        acc1[cut, :] = dot(adj[cut, 0:NODE], own[...])
        acc2[cut, :] = dot(adj[cut, NODE : NODE + HALO], stale[...])
        return c

    lax.fori_loop(0, NCH, early, 0)

    def wait_bytes(ref, sem):
        pltpu.make_async_copy(ref, ref, sem).wait()

    wait_bytes(halo.at[pl.ds(0, HALO - SLOT)], rsem.at[0])

    def first_layer(k, c):
        cut = at(k * CH, CH)
        agg = acc1[cut, :] + dot(adj[cut, NODE : NODE + HALO], halo[...])
        both[cut, F_IN : 2 * F_IN] = agg.astype(BF16)
        pre = dot(own[cut, :], w1s_ref[...]) + dot(agg.astype(BF16), w1n_ref[...])
        row = lax.broadcasted_iota(jnp.int32, (CH, HID), 0) + k * CH
        act = pre / (1.0 + jnp.exp(-pre))
        hidden[cut, :] = jnp.where(row < size, act, 0.0).astype(BF16)
        return c

    lax.fori_loop(0, NCH, first_layer, 0)

    def send_hidden(k, c):
        there = jnp.bitwise_xor(my_row, k)
        cut = at(there * CH, CH)
        send2[cut, :] = dot(pick[cut, :], hidden[...]).astype(BF16)

        def one(i, c2):
            d = there * COLS + jnp.bitwise_xor(my_col, i)

            @pl.when(d != me)
            def _():
                send_to(send2, fh_hbm, 1, d)

            return c2

        return lax.fori_loop(0, COLS, one, c)

    lax.fori_loop(0, NCH, send_hidden, 0)
    own_hidden = pltpu.make_async_copy(
        send2.at[piece_of(me)], fh_hbm.at[piece_of(me)], local_sem.at[0]
    )
    own_hidden.start()

    def second_agg(k, c):
        cut = at(k * CH, CH)
        agg2[cut, :] = (acc2[cut, :] + dot(adj[cut, 0:NODE], hidden[...])).astype(BF16)
        return c

    lax.fori_loop(0, NCH, second_agg, 0)

    gl_t[...] = jnp.zeros_like(gl_t)
    w2s_t = jnp.transpose(w2[0:HID, :])
    w2n_t = jnp.transpose(w2[HID : 2 * HID, :])

    def loss_grad(k, c):
        cut = at(k * CH, CH)
        logits = dot_nt(w2s_t, hidden[cut, :]) + dot_nt(w2n_t, agg2[cut, :])
        logits = logits[0:CLSP, :]
        cls = lax.broadcasted_iota(jnp.int32, (CLSP, CH), 0)
        logits = jnp.where(cls < CLS, logits, -jnp.inf)
        expo = jnp.exp(logits - jnp.max(logits, axis=0, keepdims=True))
        total = jnp.sum(expo, axis=0, keepdims=True)
        node = lax.broadcasted_iota(jnp.int32, (1, CH), 1) + k * CH
        weight = jnp.where((node < size) & (mask_ref[:, cut] > 0), LOSS_SCALE, 0.0)
        target = jnp.where(cls == labels_ref[:, cut], 1.0, 0.0)
        gl_t[0:CLSP, cut] = ((expo / total - target) * weight).astype(BF16)
        return c

    lax.fori_loop(0, NCH, loss_grad, 0)

    g2s = dot(gl_t[0:CLSP, :], hidden[...])
    g2n = dot(gl_t[0:CLSP, :], agg2[...])
    for b, (src, half) in enumerate(((g2s, 0), (g2s, 1), (g2n, 0), (g2n, 1))):
        contrib[512 + b * CLSP : 512 + (b + 1) * CLSP, :] = src[
            :, half * BLK : (half + 1) * BLK
        ].astype(BF16)

    def back_agg(k, c):
        cut = at(k * CH, CH)
        ga_t[:, cut] = dot(w2[HID : 2 * HID, :], gl_t[:, cut]).astype(BF16)
        return c

    lax.fori_loop(0, NCH, back_agg, 0)

    w1s_t = jnp.transpose(w1s_ref[...])
    w1n_t = jnp.transpose(w1n_ref[...])

    def back_first(k, c):
        cut = at(k * CH, CH)
        grad = dot(ga_t[...], adj[:, cut]) + dot(grad_t[...], pick[:, cut])
        grad = grad + dot(w2[0:HID, :], gl_t[:, cut])
        pre = dot_nt(w1s_t, both[cut, 0:F_IN]) + dot_nt(w1n_t, both[cut, F_IN : 2 * F_IN])
        sigma = 1.0 / (1.0 + jnp.exp(-pre))
        slope = sigma * (1.0 + pre * (1.0 - sigma))
        node = lax.broadcasted_iota(jnp.int32, (HID, CH), 1) + k * CH
        gp_t[:, cut] = jnp.where(node < size, grad * slope, 0.0).astype(BF16)
        return c

    lax.fori_loop(0, NCH, back_first, 0)

    g1 = dot(gp_t[...], both[...])
    contrib[0:HID, :] = g1[:, 0:F_IN].astype(BF16)
    contrib[HID : 2 * HID, :] = g1[:, F_IN : 2 * F_IN].astype(BF16)

    second = jnp.where(lax.rem(me, 2) == 0, -1, jnp.where(lax.rem(me - 1, 10) == 0, (me - 1) // 10, 12))
    my_piece = jnp.where(lax.rem(me, 2) == 0, me // 2, jnp.where(second < 12, 64 + second, PIECES))
    owns = my_piece < PIECES

    def send_piece(i, c):
        d = owner_of(i)

        @pl.when(d != me)
        def _():
            pltpu.make_async_remote_copy(
                src_ref=contrib.at[piece_of(i)],
                dst_ref=part_in.at[piece_of(me)],
                send_sem=ssem.at[3],
                recv_sem=rsem.at[3],
                device_id=device(d),
                device_id_type=MESH,
            ).start()

        return c

    lax.fori_loop(0, PIECES, send_piece, 0)

    @pl.when(owns)
    def _():
        part_in[piece_of(me), :] = contrib[piece_of(my_piece), :]

    def send_spread(k, c):
        there = jnp.bitwise_xor(my_row, k)
        cut = at(there * CH, CH)
        spread = dot(ga_t[...], adj[:, at(NODE + there * CH, CH)])
        spread = jnp.transpose(spread)
        live = recv_mask[cut, :] > 0.0
        for half in range(2):
            lanes = slice(half * BLK, (half + 1) * BLK)
            send3[cut, lanes] = jnp.where(live, spread[:, lanes], 0.0).astype(BF16)

        def one(i, c2):
            d = there * COLS + jnp.bitwise_xor(my_col, i)

            @pl.when(d != me)
            def _():
                send_to(send3, fg_hbm, 2, d)

            return c2

        return lax.fori_loop(0, COLS, one, c)

    send_spread(0, 0)

    @pl.when(owns)
    def _():
        wait_bytes(part_in.at[pl.ds(0, (PARTS - 1) * SLOT)], rsem.at[3])
        small[...] = jnp.zeros_like(small)

        def add(i, c):
            small[...] += part_in[piece_of(i), :].astype(F32)
            return c

        lax.fori_loop(0, PARTS, add, 0)
        result[piece_of(my_piece), :] = small[...].astype(BF16)

        def give(i, c):
            pltpu.make_async_remote_copy(
                src_ref=result.at[piece_of(my_piece)],
                dst_ref=result.at[piece_of(my_piece)],
                send_sem=ssem.at[4],
                recv_sem=rsem.at[4],
                device_id=device(jnp.bitwise_xor(me, i)),
                device_id_type=MESH,
            ).start()
            return c

        lax.fori_loop(1, PARTS, give, 0)

    lax.fori_loop(1, NCH, send_spread, 0)
    own_spread = pltpu.make_async_copy(
        send3.at[piece_of(me)], fg_hbm.at[piece_of(me)], local_sem.at[1]
    )
    own_spread.start()

    @pl.when(owns)
    def _():
        wait_bytes(part_in.at[pl.ds(0, (PARTS - 1) * SLOT)], ssem.at[4])
        wait_bytes(result.at[pl.ds(0, (PIECES - 1) * SLOT)], rsem.at[4])
        wait_bytes(contrib.at[pl.ds(0, (PIECES - 1) * SLOT)], ssem.at[3])

    @pl.when(jnp.logical_not(owns))
    def _():
        wait_bytes(result, rsem.at[4])
        wait_bytes(contrib, ssem.at[3])

    gs1_ref[...] = jnp.transpose(result[0:HID, :].astype(F32))
    gn1_ref[...] = jnp.transpose(result[HID : 2 * HID, :].astype(F32))
    for b, (dst, half) in enumerate(((gs2_ref, 0), (gs2_ref, 1), (gn2_ref, 0), (gn2_ref, 1))):
        block = result[512 + b * CLSP : 512 + (b + 1) * CLSP, :].astype(F32)
        block = jnp.concatenate([block, jnp.zeros((HID - CLSP, BLK), F32)], axis=0)
        dst[half * BLK : (half + 1) * BLK, :] = jnp.transpose(block)[:, 0:CLS]

    own_hidden.wait()
    own_spread.wait()
    wait_bytes(send1.at[pl.ds(0, HALO - SLOT)], ssem.at[0])
    for which, src, dst in ((1, send2, fh_hbm), (2, send3, fg_hbm)):
        wait_bytes(src.at[pl.ds(0, HALO - SLOT)], ssem.at[which])
        wait_bytes(dst.at[pl.ds(0, HALO - SLOT)], rsem.at[which])


def local(
    features, self_one, neigh_one, self_two, neigh_two, tile_values, tile_rows, tile_cols,
    tile_count, part_size, send_rows, send_count, labels, train_mask, stale_hidden, stale_grads,
):
    index = jnp.arange(TILES)
    live = index < tile_count[0]
    block = tile_rows[0] * 32 + tile_cols[0]
    later = (block[:, None] == block[None, :]) & (index[None, :] > index[:, None]) & live[None, :]
    nxt = jnp.min(jnp.where(later, index[None, :], TILES), axis=1).astype(jnp.int32)
    here = (jnp.arange(512)[:, None] == block[None, :]) & live[None, :]
    first = jnp.min(jnp.where(here, index[None, :], TILES), axis=1).astype(jnp.int32)

    smem = pl.BlockSpec(memory_space=pltpu.SMEM)
    vmem = pl.BlockSpec(memory_space=pltpu.VMEM)
    hbm = pl.BlockSpec(memory_space=pl.ANY)
    outs = pl.pallas_call(
        kernel,
        out_shape=(
            jax.ShapeDtypeStruct((F_IN, HID), F32),
            jax.ShapeDtypeStruct((F_IN, HID), F32),
            jax.ShapeDtypeStruct((HID, CLS), F32),
            jax.ShapeDtypeStruct((HID, CLS), F32),
            jax.ShapeDtypeStruct((HALO, HID), BF16),
            jax.ShapeDtypeStruct((HALO, HID), BF16),
        ),
        in_specs=[smem] * 3 + [hbm] * 4 + [vmem] * 8,
        out_specs=(vmem, vmem, vmem, vmem, hbm, hbm),
        scratch_shapes=[
            pltpu.VMEM((NODE, NODE + HALO), BF16),
            pltpu.VMEM((HALO, NODE), BF16),
            pltpu.VMEM((TILES + 1, BLK, BLK), F32),
            pltpu.VMEM((2, 48, BLK, BLK), BF16),
            pltpu.VMEM((NODE, F_IN), BF16),
            pltpu.VMEM((NODE, 2 * F_IN), BF16),
            pltpu.VMEM((HALO, F_IN), BF16),
            pltpu.VMEM((NODE, HID), BF16),
            pltpu.VMEM((HALO, HID), BF16),
            pltpu.VMEM((HID, HALO), BF16),
            pltpu.VMEM((NODE, F_IN), F32),
            pltpu.VMEM((NODE, HID), F32),
            pltpu.VMEM((NODE, HID), BF16),
            pltpu.VMEM((HID, NODE), BF16),
            pltpu.VMEM((HID, NODE), BF16),
            pltpu.VMEM((HID, NODE), BF16),
            pltpu.VMEM((HALO, BLK), F32),
            pltpu.VMEM((HALO, F_IN), BF16),
            pltpu.VMEM((HALO, HID), BF16),
            pltpu.VMEM((HALO, HID), BF16),
            pltpu.VMEM((2 * HID, HID), BF16),
            pltpu.VMEM((PIECES * SLOT, BLK), BF16),
            pltpu.VMEM((PARTS * SLOT, BLK), BF16),
            pltpu.VMEM((PIECES * SLOT, BLK), BF16),
            pltpu.VMEM((SLOT, BLK), F32),
            pltpu.SemaphoreType.DMA((2,)),
            pltpu.SemaphoreType.DMA((3,)),
            pltpu.SemaphoreType.DMA((5,)),
            pltpu.SemaphoreType.DMA((5,)),
            pltpu.SemaphoreType.DMA((2,)),
        ],
        compiler_params=pltpu.CompilerParams(
            collective_id=0, has_side_effects=True, vmem_limit_bytes=62 * 1024 * 1024
        ),
        cost_estimate=pl.CostEstimate(
            flops=20_000_000_000, bytes_accessed=14_000_000, transcendentals=2_000_000
        ),
        name="train_step",
    )(
        nxt, first, part_size,
        features, tile_values, stale_hidden, stale_grads,
        self_one, neigh_one, self_two, neigh_two, send_rows[0], send_count,
        labels.reshape(1, NODE), train_mask.reshape(1, NODE),
    )
    return tuple(outs)


def solution(mesh):
    part = P(("row", "col"))
    return jax.shard_map(
        local,
        mesh=mesh,
        in_specs=(
            part, P(), P(), P(), P(), part, part, part, part, part, part, P(), part, part, part, part,
        ),
        out_specs=(P(), P(), P(), P(), part, part),
        check_vma=False,
    )
```

profile of v0, /device:TPU:1, one launch (start us, length us, event | category | flops | bytes accessed | tf_op | source)
XLA Modules:
  0.0 113.6 jit_solution(6995487918868818840)
XLA Ops:
  1.9 0.7 multiply_add_fusion
  2.6 0.8 select_reduce_fusion.1.nxt
  3.4 0.7 select_reduce_fusion.first
  4.1 1.4 %copy.27 = s32[1,128,16]{2,1,0:T(8,128)} copy(s32[1,128,16]{1,2,0:T(8,128)} %param.26) | data formatting | bytes 16384 | tf_op args[10]
  5.6 1.6 %copy.28.w2s_ref = bf16[256,172]{1,0:T(8,128)(2,1)} copy(bf16[256,172]{0,1:T(8,128)(2,1)} %param.19) | data formatting | bytes 176128 | tf_op args[3]
  7.2 1.6 %copy.29.w2n_ref = bf16[256,172]{1,0:T(8,128)(2,1)} copy(bf16[256,172]{0,1:T(8,128)(2,1)} %param.20) | data formatting | bytes 176128 | tf_op args[4]
  8.9 93.6 %train_step.1 = (f32[128,256]{1,0:T(8,128)}, f32[128,256]{1,0:T(8,128)}, f32[256,172]{1,0:T(8,128)}, f32[256,172]{1,0:T(8,128)}, bf16[2048,256]{1,0:T(8,128)(2,1)}, /*index=5*/bf16[2048,256]{1,0:T(8,128)(2,1)}) custom-call(s32[192]{0:T(256)} %select_reduce_fusion.1.nxt, s32[512]{0:T(512)} %select_reduce_fusion.first, s32[1]{0:T(128)S(6)} %copy.37.size_ref, ...), custom_call_target="tpu_custom_call" | custom-call | flops 20000000000 | bytes 14000000 | tf_op jit(solution)/shard_map/train_step/pallas_call | solution.py:435
  102.5 1.7 %copy.30 = f32[256,172]{0,1:T(8,128)} copy(f32[256,172]{1,0:T(8,128)} %get-tuple-element.14) | data formatting | bytes 352256 | tf_op jit(solution)/shard_map/train_step/pallas_call | solution.py:435
  104.2 1.7 %copy.31 = f32[256,172]{0,1:T(8,128)} copy(f32[256,172]{1,0:T(8,128)} %get-tuple-element.15) | data formatting | bytes 352256 | tf_op jit(solution)/shard_map/train_step/pallas_call | solution.py:435
  106.0 1.6 %copy.38 = f32[128,256]{1,0:T(8,128)} copy(f32[128,256]{1,0:T(8,128)} %get-tuple-element.24) | data formatting | bytes 262144
  107.5 1.6 %copy.39 = f32[128,256]{1,0:T(8,128)} copy(f32[128,256]{1,0:T(8,128)} %get-tuple-element.25) | data formatting | bytes 262144
  109.1 2.3 %copy.40 = bf16[2048,256]{1,0:T(8,128)(2,1)} copy(bf16[2048,256]{1,0:T(8,128)(2,1)} %get-tuple-element.28) | data formatting | bytes 2097152
  111.4 2.3 %copy.41 = bf16[2048,256]{1,0:T(8,128)(2,1)} copy(bf16[2048,256]{1,0:T(8,128)(2,1)} %get-tuple-element.29) | data formatting | bytes 2097152
  (1 shorter events, 0.0 us)
where the time goes:
time: 114 us
  Pallas kernels  93.6 us (82%)
  local copies, waits for them, and re-layouts  15.8 us (14%)
  other arithmetic  2.22 us (2%)
  between operations  1.94 us (2%)
    pallas_call x1, Pallas kernels, local(): pl.pallas_call(kernel, out_shape=(jax.ShapeDtypeStruct((F_IN, HID), F32),...  93.6 us
    unnamed x7, local copies, waits for them, and re-layouts  12.4 us
    pallas_call x2, local copies, waits for them, and re-layouts, local(): pl.pallas_call(kernel, out_shape=(jax.ShapeDtypeStruct((F_IN, HID), F32),...  3.47 us

commit v1 on v0

v1 whole, which is shorter than its diff:
```python
import jax
import jax.numpy as jnp
from jax import lax
from jax.experimental import pallas as pl
from jax.experimental.pallas import tpu as pltpu
from jax.sharding import PartitionSpec as P

MESH = pl.DeviceIdType.MESH
F32 = jnp.float32
BF16 = jnp.bfloat16
NODE = 2048
HALF = 1024
HALO = 2048
BLK = 128
SLOT = 16
PARTS = 128
COLS = 32
TILES = 192
STAGE = 48
F_IN = 128
HID = 256
CLS = 172
CLSP = 176
CH = 512
NCH = 4
PIECE = 48
SIDE = 16 * PIECE
LOSS_SCALE = 1.0 / 32.0


def dot(a, b):
    return lax.dot_general(a, b, (((1,), (0,)), ((), ())), preferred_element_type=F32)


def dot_nt(a, b):
    return lax.dot_general(a, b, (((1,), (1,)), ((), ())), preferred_element_type=F32)


def at(start, size):
    return pl.ds(pl.multiple_of(start, size), size)


def device(index):
    return (index >> 5, index & 31)


def offset(s):
    k, dx, dy, core = s >> 5, (s >> 3) & 3, (s >> 1) & 3, s & 1
    dz = k ^ dx ^ dy
    return (dx << 5) + (dy << 3) + (dz << 1) + core


def choose(upper, wide):
    width = wide.shape[1] // 2
    cuts = []
    for b in range(width // BLK):
        low = wide[:, b * BLK : (b + 1) * BLK]
        high = wide[:, width + b * BLK : width + (b + 1) * BLK]
        cuts.append(jnp.where(upper, high, low))
    return cuts[0] if len(cuts) == 1 else jnp.concatenate(cuts, axis=1)


def prepare(
    rows_s, cols_s, count_s, size_s, tiles_hbm, feat_hbm, rows_hbm, count_hbm,
    adj, pick, own, send1, upper_ref, recv_ref,
    tbuf, sums, own_wide, rows_ref, count_ref, state, slot_block, tile_sem, load_sem,
):
    me = lax.axis_index("row") * COLS + lax.axis_index("col")
    size = size_s[0]
    used = count_s[0]

    load_rows = pltpu.make_async_copy(rows_hbm, rows_ref, load_sem.at[1])
    load_rows.start()
    load_count = pltpu.make_async_copy(count_hbm, count_ref, load_sem.at[2])
    load_count.start()
    load_own = pltpu.make_async_copy(feat_hbm, own, load_sem.at[0])
    load_own.start()

    def load_tiles(k):
        cut = pl.ds(k * STAGE, STAGE)
        return pltpu.make_async_copy(tiles_hbm.at[cut], tbuf.at[cut], tile_sem.at[k])

    for k in range(TILES // STAGE):
        load_tiles(k).start()

    load_rows.wait()
    load_count.wait()

    part = lax.broadcasted_iota(jnp.int32, (PARTS, BLK), 0)
    is_me = jnp.where(part == me, 1.0, 0.0).astype(BF16)
    counts = count_ref[...].astype(F32)
    in_count = dot(counts.astype(BF16), is_me).astype(BF16)
    out_count = dot(jnp.transpose(counts).astype(BF16), is_me).astype(BF16)
    rows = rows_ref[...]
    high = (rows >> 7).astype(F32).astype(BF16)
    low = (rows & 127).astype(F32).astype(BF16)
    ones = jnp.ones((SLOT, BLK), BF16)

    def build_pick(k, c):
        cut = at(k * CH, CH)
        h = lax.broadcasted_iota(jnp.int32, (CH, PARTS), 0) + k * CH
        q = lax.broadcasted_iota(jnp.int32, (CH, PARTS), 1)
        expand = jnp.where((offset(h >> 4) ^ me) == q, 1.0, 0.0).astype(BF16)
        hs = lax.broadcasted_iota(jnp.int32, (CH, SLOT), 0)
        js = lax.broadcasted_iota(jnp.int32, (CH, SLOT), 1)
        slot_is = (hs & 15) == js
        high_b = dot(jnp.where(slot_is, dot_nt(expand, high), 0.0).astype(BF16), ones)
        low_b = dot(jnp.where(slot_is, dot_nt(expand, low), 0.0).astype(BF16), ones)
        j_of = (h & 15).astype(F32)
        live = j_of < dot(expand, out_count)
        upper = high_b >= 8.0
        upper_ref[cut, :] = jnp.where(upper, 1.0, 0.0).astype(BF16)
        key = jnp.where(upper, high_b - 8.0, high_b)
        key = jnp.where(live & (low_b == q.astype(F32)), key, -1.0)
        for b in range(HALF // BLK):
            pick[cut, b * BLK : (b + 1) * BLK] = jnp.where(key == float(b), 1.0, 0.0).astype(BF16)
        natural = jnp.where((h >> 4) == q, 1.0, 0.0).astype(BF16)
        recv_ref[cut, :] = jnp.where(j_of < dot(natural, in_count), 1.0, 0.0).astype(BF16)
        return c

    lax.fori_loop(0, NCH, build_pick, 0)

    load_own.wait()

    def mask_own(k, c):
        cut = at(k * CH, CH)
        row = lax.broadcasted_iota(jnp.int32, (CH, F_IN), 0) + k * CH
        kept = jnp.where(row < size, own[cut, :].astype(F32), 0.0).astype(BF16)
        own[cut, :] = kept
        own_wide[at((k & 1) * CH, CH), at((k >> 1) * F_IN, F_IN)] = kept
        return c

    lax.fori_loop(0, NCH, mask_own, 0)

    def gather_feats(k, c):
        cut = at(k * CH, CH)
        both_halves = dot(pick[cut, :], own_wide[...])
        upper = upper_ref[cut, :].astype(F32) > 0.0
        send1[cut, :] = choose(upper, both_halves).astype(BF16)
        return c

    lax.fori_loop(0, NCH, gather_feats, 0)

    def clear(i, c):
        adj[at(i * BLK, BLK), :] = jnp.zeros((BLK, NODE + HALO), BF16)
        return c

    lax.fori_loop(0, NODE // BLK, clear, 0)

    def clear_state(i, c):
        state[i] = 0
        return c

    lax.fori_loop(0, 512, clear_state, 0, unroll=8)
    state[512] = 0

    def place(t, c):
        r, col = rows_s[0, t], cols_s[0, t]
        block = r * 32 + col
        known = state[block]
        where = (at(r * BLK, BLK), at(col * BLK, BLK))

        @pl.when(known == 0)
        def _():
            adj[where] = tbuf[t]
            state[block] = 1

        @pl.when(known == 1)
        def _():
            slot = state[512]
            sums[slot] = adj[where].astype(F32) + tbuf[t].astype(F32)
            slot_block[slot] = block
            state[block] = slot + 2
            state[512] = slot + 1

        @pl.when(known > 1)
        def _():
            sums[known - 2] += tbuf[t].astype(F32)

        return c

    for k in range(TILES // STAGE):
        load_tiles(k).wait()
        lax.fori_loop(k * STAGE, jnp.clip(used, k * STAGE, (k + 1) * STAGE), place, 0)

    def settle(slot, c):
        block = slot_block[slot]
        adj[at((block >> 5) * BLK, BLK), at((block & 31) * BLK, BLK)] = sums[slot].astype(BF16)
        return c

    lax.fori_loop(0, state[512], settle, 0)


def step(
    size_ref, stale_hbm, grads_hbm,
    adj, pick, own, send1, upper_ref, recv_ref,
    w1s_ref, w1n_ref, w2s_ref, w2n_ref, labels_ref, mask_ref,
    gs1_ref, gn1_ref, gs2_ref, gn2_ref, fh_hbm, fg_hbm,
    both, agg_wide, halo, two, stale, grads, grad_t, acc1, acc2,
    gl_t, ga_t, gp_t, send2, agg_in, send3, w1, w2, fresh_buf,
    contrib, pair_in, pair_sum, plane_in, z_in, result,
    load_sem, ssem, rsem, local_sem,
):
    my_row = lax.axis_index("row")
    my_col = lax.axis_index("col")
    me = my_row * COLS + my_col
    my_y, my_zc = my_col >> 3, my_col & 7
    my_z, my_core = (my_col >> 1) & 3, my_col & 1
    my_xy = my_row * 4 + my_y
    size = size_ref[0]

    barrier = pltpu.get_barrier_semaphore()

    def greet(i, c):
        pl.semaphore_signal(
            barrier, inc=1, device_id=device(me ^ i), device_id_type=MESH
        )
        return c

    lax.fori_loop(1, PARTS, greet, 0)

    load_grads = pltpu.make_async_copy(grads_hbm, grads, load_sem.at[0])
    load_grads.start()
    load_stale = pltpu.make_async_copy(stale_hbm, stale, load_sem.at[1])
    load_stale.start()

    w1[0:F_IN, :] = w1s_ref[...]
    w1[F_IN : 2 * F_IN, :] = w1n_ref[...]
    w2[...] = jnp.zeros_like(w2)
    w2[0:CLS, 0:HID] = w2s_ref[...]
    w2[0:CLS, HID : 2 * HID] = w2n_ref[...]

    def piece_of(index):
        return at(index * SLOT, SLOT)

    def send_to(src, at_piece, dst, which, d):
        pltpu.make_async_remote_copy(
            src_ref=src.at[piece_of(at_piece)],
            dst_ref=dst.at[piece_of(me)],
            send_sem=ssem.at[which],
            recv_sem=rsem.at[which],
            device_id=device(d),
            device_id_type=MESH,
        ).start()

    def wait_bytes(ref, sem):
        pltpu.make_async_copy(ref, ref, sem).wait()

    pl.semaphore_wait(barrier, PARTS - 1)

    def send_feats(i, c):
        send_to(send1, i, halo, 0, me ^ offset(i))
        return c

    lax.fori_loop(1, PARTS, send_feats, 0)
    halo[piece_of(me), :] = jnp.zeros((SLOT, F_IN), BF16)

    def early_own(k, c):
        cut = at(k * CH, CH)
        both[cut, 0:F_IN] = own[cut, :]
        acc1[cut, :] = dot(adj[cut, 0:NODE], own[...])
        return c

    lax.fori_loop(0, NCH, early_own, 0)

    load_stale.wait()

    def mask_stale(k, c):
        cut = at(k * CH, CH)
        live = recv_ref[cut, :].astype(F32) > 0.0
        for half in range(2):
            lanes = slice(half * BLK, (half + 1) * BLK)
            stale[cut, lanes] = jnp.where(live, stale[cut, lanes].astype(F32), 0.0).astype(BF16)
        return c

    lax.fori_loop(0, NCH, mask_stale, 0)

    def early_stale(k, c):
        cut = at(k * CH, CH)
        acc2[cut, :] = dot(adj[cut, NODE : NODE + HALO], stale[...])
        return c

    lax.fori_loop(0, NCH, early_stale, 0)

    load_grads.wait()

    def order_grads(i, c):
        send3[piece_of(i), :] = grads[piece_of(me ^ offset(i)), :]
        return c

    lax.fori_loop(0, PARTS, order_grads, 0, unroll=8)

    def turn_grads(k, c):
        cut = at(k * CH, CH)
        upper = upper_ref[cut, :].astype(F32) > 0.0
        value = send3[cut, :].astype(F32)
        upper = jnp.concatenate([upper, upper], axis=1)
        grad_t[0, :, cut] = jnp.transpose(jnp.where(upper, 0.0, value).astype(BF16))
        grad_t[1, :, cut] = jnp.transpose(jnp.where(upper, value, 0.0).astype(BF16))
        return c

    lax.fori_loop(0, NCH, turn_grads, 0)

    wait_bytes(halo.at[pl.ds(0, HALO - SLOT)], rsem.at[0])

    def first_agg(k, c):
        cut = at(k * CH, CH)
        agg = (acc1[cut, :] + dot(adj[cut, NODE : NODE + HALO], halo[...])).astype(BF16)
        both[cut, F_IN : 2 * F_IN] = agg
        agg_wide[at((k & 1) * CH, CH), at((k >> 1) * F_IN, F_IN)] = agg
        return c

    lax.fori_loop(0, NCH, first_agg, 0)

    def send_agg(k, c):
        cut = at(k * CH, CH)
        upper = upper_ref[cut, :].astype(F32) > 0.0
        send2[cut, :] = choose(upper, dot(pick[cut, :], agg_wide[...])).astype(BF16)

        def one(i, c2):
            @pl.when(i > 0)
            def _():
                send_to(send2, i, agg_in, 1, me ^ offset(i))

            return c2

        return lax.fori_loop(k * COLS, (k + 1) * COLS, one, c)

    lax.fori_loop(0, NCH, send_agg, 0)
    agg_in[piece_of(me), :] = jnp.zeros((SLOT, F_IN), BF16)

    def first_layer(k, c):
        cut = at(k * CH, CH)
        pre = dot(both[cut, :], w1[...])
        row = lax.broadcasted_iota(jnp.int32, (CH, HID), 0) + k * CH
        act = pre / (1.0 + jnp.exp(-pre))
        two[cut, 0:HID] = jnp.where(row < size, act, 0.0).astype(BF16)
        return c

    lax.fori_loop(0, NCH, first_layer, 0)

    def second_agg(k, c):
        cut = at(k * CH, CH)
        agg = acc2[cut, :] + dot(adj[cut, 0:NODE], two[:, 0:HID])
        two[cut, HID : 2 * HID] = agg.astype(BF16)
        return c

    lax.fori_loop(0, NCH, second_agg, 0)

    gl_t[CLSP:HID, :] = jnp.zeros((HID - CLSP, NODE), BF16)

    def loss_grad(k, c):
        cut = at(k * CH, CH)
        logits = dot_nt(w2[0:CLSP, :], two[cut, :])
        cls = lax.broadcasted_iota(jnp.int32, (CLSP, CH), 0)
        logits = jnp.where(cls < CLS, logits, -jnp.inf)
        expo = jnp.exp(logits - jnp.max(logits, axis=0, keepdims=True))
        total = jnp.sum(expo, axis=0, keepdims=True)
        node = lax.broadcasted_iota(jnp.int32, (1, CH), 1) + k * CH
        weight = jnp.where((node < size) & (mask_ref[:, cut] > 0), LOSS_SCALE, 0.0)
        target = jnp.where(cls == labels_ref[:, cut], 1.0, 0.0)
        gl_t[0:CLSP, cut] = ((expo * (1.0 / total) - target) * weight).astype(BF16)
        return c

    lax.fori_loop(0, NCH, loss_grad, 0)

    w2s = jnp.transpose(w2[:, 0:HID])
    w2n = jnp.transpose(w2[:, HID : 2 * HID])

    def back_agg(k, c):
        cut = at(k * CH, CH)
        ga_t[:, cut] = dot(w2n, gl_t[:, cut]).astype(BF16)
        return c

    lax.fori_loop(0, NCH, back_agg, 0)

    def block_at(dx, k):
        return (my_row ^ dx) * 4 + (my_y ^ dx ^ k)

    def make_spread(k):
        for pair in range(2):
            blocks = [block_at(2 * pair, k), block_at(2 * pair + 1, k)]
            cols = [adj[:, at(NODE + b * BLK, BLK)] for b in blocks]
            spread = jnp.transpose(dot(ga_t[...], jnp.concatenate(cols, axis=1)))
            for b, part in zip(blocks, (spread[0:BLK], spread[BLK : 2 * BLK])):
                cut = at(b * BLK, BLK)
                live = recv_ref[cut, :].astype(F32) > 0.0
                for half in range(2):
                    lanes = slice(half * BLK, (half + 1) * BLK)
                    send3[cut, lanes] = jnp.where(live, part[:, lanes], 0.0).astype(BF16)

    def send_spread(k):
        def one(i, c):
            d = block_at(i & 3, k) * 8 + (my_zc ^ (i >> 2))

            @pl.when(d != me)
            def _():
                send_to(send3, d, fg_hbm, 2, d)

            return c

        lax.fori_loop(0, COLS, one, 0)

    def part_copy(which, src, dst, d):
        pltpu.make_async_remote_copy(
            src_ref=src,
            dst_ref=dst,
            send_sem=ssem.at[which],
            recv_sem=rsem.at[which],
            device_id=device(d),
            device_id_type=MESH,
        ).start()

    mine = at(my_core * SIDE, SIDE)
    other = at((1 - my_core) * SIDE, SIDE)
    home = at(my_core * SIDE + my_xy * PIECE, PIECE)

    def plane_peer(i):
        return me ^ ((i >> 2) << 5) ^ ((i & 3) << 3)

    def plane_index(d):
        return (d >> 5) * 4 + ((d >> 3) & 3)

    def reduce_pair():
        part_copy(3, contrib.at[other], pair_in, me ^ 1)

    def reduce_plane():
        wait_bytes(pair_in, rsem.at[3])
        pair_sum[...] = (contrib[mine, :].astype(F32) + pair_in[...].astype(F32)).astype(BF16)

        def one(i, c):
            d = plane_peer(i)
            part_copy(
                4, pair_sum.at[at(plane_index(d) * PIECE, PIECE)],
                plane_in.at[at(my_xy * PIECE, PIECE)], d,
            )
            return c

        lax.fori_loop(1, 16, one, 0)

    def reduce_z():
        wait_bytes(plane_in.at[pl.ds(0, 15 * PIECE)], rsem.at[4])
        plane_in[at(my_xy * PIECE, PIECE), :] = pair_sum[at(my_xy * PIECE, PIECE), :]
        z_in[at(my_z * PIECE, PIECE), :] = jnp.sum(
            plane_in[...].astype(F32).reshape(16, PIECE, BLK), axis=0
        ).astype(BF16)
        for i in range(1, 4):
            cut = at(my_z * PIECE, PIECE)
            part_copy(5, z_in.at[cut], z_in.at[cut], me ^ (i << 1))

    def return_plane():
        wait_bytes(z_in.at[pl.ds(0, 3 * PIECE)], rsem.at[5])
        result[home, :] = jnp.sum(
            z_in[...].astype(F32).reshape(4, PIECE, BLK), axis=0
        ).astype(BF16)

        def one(i, c):
            part_copy(6, result.at[home], result.at[home], plane_peer(i))
            return c

        lax.fori_loop(1, 16, one, 0)

    def return_pair():
        wait_bytes(result.at[pl.ds(0, 15 * PIECE)], rsem.at[6])
        part_copy(7, result.at[mine], result.at[mine], me ^ 1)

    contrib[...] = jnp.zeros_like(contrib)
    g2 = dot(gl_t[0:CLSP, :], two[...])
    for b in range(4):
        contrib[2 * HID + b * CLSP : 2 * HID + (b + 1) * CLSP, :] = g2[
            :, b * BLK : (b + 1) * BLK
        ].astype(BF16)

    w1_t = jnp.transpose(w1[...])

    def back_first(k, c):
        cut = at(k * CH, CH)
        grad = dot(ga_t[...], adj[:, cut]) + dot(grad_t[k >> 1], pick[:, at((k & 1) * CH, CH)])
        grad = grad + dot(w2s, gl_t[:, cut])
        pre = dot_nt(w1_t, both[cut, :])
        sigma = 1.0 / (1.0 + jnp.exp(-pre))
        slope = sigma * (1.0 + pre * (1.0 - sigma))
        node = lax.broadcasted_iota(jnp.int32, (HID, CH), 1) + k * CH
        gp_t[:, cut] = jnp.where(node < size, grad * slope, 0.0).astype(BF16)
        return c

    make_spread(0)
    send_spread(0)
    lax.fori_loop(0, 2, back_first, 0)
    make_spread(1)
    send_spread(1)
    lax.fori_loop(2, NCH, back_first, 0)

    g1 = dot(gp_t[...], both[...])
    contrib[0:HID, :] = g1[:, 0:F_IN].astype(BF16)
    contrib[HID : 2 * HID, :] = g1[:, F_IN : 2 * F_IN].astype(BF16)
    reduce_pair()
    make_spread(2)
    reduce_plane()
    send_spread(2)
    make_spread(3)
    reduce_z()
    send_spread(3)
    own_spread = pltpu.make_async_copy(
        send3.at[piece_of(me)], fg_hbm.at[piece_of(me)], local_sem.at[0]
    )
    own_spread.start()

    wait_bytes(agg_in.at[pl.ds(0, HALO - SLOT)], rsem.at[1])

    def fresh(k, c):
        cut = at(k * CH, CH)
        pre = dot(halo[cut, :], w1[0:F_IN, :]) + dot(agg_in[cut, :], w1[F_IN : 2 * F_IN, :])
        fresh_buf[cut, :] = (pre / (1.0 + jnp.exp(-pre))).astype(BF16)
        return c

    lax.fori_loop(0, NCH, fresh, 0)
    give_fresh = pltpu.make_async_copy(fresh_buf, fh_hbm, local_sem.at[1])
    give_fresh.start()

    return_plane()
    return_pair()
    wait_bytes(result.at[other], rsem.at[7])

    gs1_ref[...] = jnp.transpose(result[0:HID, :].astype(F32))
    gn1_ref[...] = jnp.transpose(result[HID : 2 * HID, :].astype(F32))
    for b, (dst, half) in enumerate(((gs2_ref, 0), (gs2_ref, 1), (gn2_ref, 0), (gn2_ref, 1))):
        block = result[2 * HID + b * CLSP : 2 * HID + (b + 1) * CLSP, :].astype(F32)
        dst[:, half * BLK : (half + 1) * BLK] = block[0:CLS, :]

    wait_bytes(send1.at[pl.ds(0, HALO - SLOT)], ssem.at[0])
    wait_bytes(send2.at[pl.ds(0, HALO - SLOT)], ssem.at[1])
    wait_bytes(send3.at[pl.ds(0, HALO - SLOT)], ssem.at[2])
    wait_bytes(contrib.at[mine], ssem.at[3])
    wait_bytes(plane_in.at[pl.ds(0, 15 * PIECE)], ssem.at[4])
    wait_bytes(z_in.at[pl.ds(0, 3 * PIECE)], ssem.at[5])
    wait_bytes(result.at[pl.ds(0, 15 * PIECE)], ssem.at[6])
    wait_bytes(result.at[mine], ssem.at[7])
    own_spread.wait()
    give_fresh.wait()
    wait_bytes(fg_hbm.at[pl.ds(0, HALO - SLOT)], rsem.at[2])


def hand_over(*refs):
    held, sems = refs[12:18], refs[18]
    into = [pltpu.make_async_copy(refs[i], held[i], sems.at[i]) for i in range(6)]
    out = [pltpu.make_async_copy(held[i], refs[6 + i], sems.at[6 + i]) for i in range(6)]
    for copy in into[::-1]:
        copy.start()
    for i in range(5, -1, -1):
        into[i].wait()
        out[i].start()
    for copy in out:
        copy.wait()


def local(
    features, self_one, neigh_one, self_two, neigh_two, tile_values, tile_rows, tile_cols,
    tile_count, part_size, send_rows, send_count, labels, train_mask, stale_hidden, stale_grads,
):
    def in_hbm(x):
        return pltpu.with_memory_space_constraint(x, pltpu.HBM)

    smem = pl.BlockSpec(memory_space=pltpu.SMEM)
    vmem = pl.BlockSpec(memory_space=pltpu.VMEM)
    hbm = pl.BlockSpec(memory_space=pltpu.HBM)
    anywhere = pl.BlockSpec(memory_space=pl.ANY)
    packed = pl.pallas_call(
        prepare,
        out_shape=(
            jax.ShapeDtypeStruct((NODE, NODE + HALO), BF16),
            jax.ShapeDtypeStruct((HALO, HALF), BF16),
            jax.ShapeDtypeStruct((NODE, F_IN), BF16),
            jax.ShapeDtypeStruct((HALO, F_IN), BF16),
            jax.ShapeDtypeStruct((HALO, BLK), BF16),
            jax.ShapeDtypeStruct((HALO, BLK), BF16),
        ),
        in_specs=[smem] * 4 + [hbm] * 4,
        out_specs=(vmem,) * 6,
        scratch_shapes=[
            pltpu.VMEM((TILES, BLK, BLK), BF16),
            pltpu.VMEM((TILES // 2, BLK, BLK), F32),
            pltpu.VMEM((HALF, 2 * F_IN), BF16),
            pltpu.VMEM((SLOT, PARTS), jnp.int32),
            pltpu.VMEM((PARTS, PARTS), jnp.int32),
            pltpu.SMEM((520,), jnp.int32),
            pltpu.SMEM((TILES // 2,), jnp.int32),
            pltpu.SemaphoreType.DMA((TILES // STAGE,)),
            pltpu.SemaphoreType.DMA((3,)),
        ],
        compiler_params=pltpu.CompilerParams(vmem_limit_bytes=20 * 1024 * 1024),
        cost_estimate=pl.CostEstimate(
            flops=1_500_000_000, bytes_accessed=8_000_000, transcendentals=0
        ),
        name="prepare",
    )(
        in_hbm(tile_rows), in_hbm(tile_cols), tile_count, part_size,
        *(in_hbm(x) for x in (tile_values, features, send_rows[0].T, send_count)),
    )
    outs = pl.pallas_call(
        step,
        out_shape=(
            jax.ShapeDtypeStruct((F_IN, HID), F32),
            jax.ShapeDtypeStruct((F_IN, HID), F32),
            jax.ShapeDtypeStruct((CLS, HID), F32),
            jax.ShapeDtypeStruct((CLS, HID), F32),
            jax.ShapeDtypeStruct((HALO, HID), BF16),
            jax.ShapeDtypeStruct((HALO, HID), BF16),
        ),
        in_specs=[smem] + [hbm] * 2 + [vmem] * 12,
        out_specs=(vmem,) * 4 + (anywhere,) * 2,
        scratch_shapes=[
            pltpu.VMEM((NODE, 2 * F_IN), BF16),
            pltpu.VMEM((HALF, 2 * F_IN), BF16),
            pltpu.VMEM((HALO, F_IN), BF16),
            pltpu.VMEM((NODE, 2 * HID), BF16),
            pltpu.VMEM((HALO, HID), BF16),
            pltpu.VMEM((HALO, HID), BF16),
            pltpu.VMEM((2, HID, HALO), BF16),
            pltpu.VMEM((NODE, F_IN), F32),
            pltpu.VMEM((NODE, HID), F32),
            pltpu.VMEM((HID, NODE), BF16),
            pltpu.VMEM((HID, NODE), BF16),
            pltpu.VMEM((HID, NODE), BF16),
            pltpu.VMEM((HALO, F_IN), BF16),
            pltpu.VMEM((HALO, F_IN), BF16),
            pltpu.VMEM((HALO, HID), BF16),
            pltpu.VMEM((2 * F_IN, HID), BF16),
            pltpu.VMEM((HID, 2 * HID), BF16),
            pltpu.VMEM((HALO, HID), BF16),
            pltpu.VMEM((2 * SIDE, BLK), BF16),
            pltpu.VMEM((SIDE, BLK), BF16),
            pltpu.VMEM((SIDE, BLK), BF16),
            pltpu.VMEM((SIDE, BLK), BF16),
            pltpu.VMEM((4 * PIECE, BLK), BF16),
            pltpu.VMEM((2 * SIDE, BLK), BF16),
            pltpu.SemaphoreType.DMA((2,)),
            pltpu.SemaphoreType.DMA((8,)),
            pltpu.SemaphoreType.DMA((8,)),
            pltpu.SemaphoreType.DMA((2,)),
        ],
        compiler_params=pltpu.CompilerParams(
            collective_id=0, has_side_effects=True, vmem_limit_bytes=23 * 1024 * 1024
        ),
        cost_estimate=pl.CostEstimate(
            flops=20_000_000_000, bytes_accessed=8_000_000, transcendentals=2_000_000
        ),
        name="train_step",
    )(
        part_size, in_hbm(stale_hidden), in_hbm(stale_grads), *packed,
        self_one, neigh_one, self_two.T, neigh_two.T,
        labels.reshape(1, NODE), train_mask.reshape(1, NODE),
    )
    gs1, gn1, gs2, gn2, fresh_hidden, fresh_grads = pl.pallas_call(
        hand_over,
        out_shape=tuple(jax.ShapeDtypeStruct(o.shape, o.dtype) for o in outs),
        in_specs=[anywhere] * 6,
        out_specs=(anywhere,) * 6,
        scratch_shapes=[pltpu.VMEM(o.shape, o.dtype) for o in outs] + [pltpu.SemaphoreType.DMA((12,))],
        name="hand_over",
    )(*(in_hbm(o) for o in outs))
    return (gs1, gn1, gs2.T, gn2.T, fresh_hidden, fresh_grads)


def solution(mesh):
    part = P(("row", "col"))
    return jax.shard_map(
        local,
        mesh=mesh,
        in_specs=(
            part, P(), P(), P(), P(), part, part, part, part, part, part, P(), part, part, part, part,
        ),
        out_specs=(P(), P(), P(), P(), part, part),
        check_vma=False,
    )
```

time: 114 us -> 91.3 us (0.80)
  local copies, waits for them, and re-layouts: 15.8 us -> 4.64 us
  Pallas kernels: 93.6 us -> 84.3 us
  other arithmetic: 2.22 us -> 0 us
    pallas_call x1 -> x3, Pallas kernels: 93.6 us -> 84.3 us  [the longest x1 69.2 us: local(): pl.pallas_call(step, out_shape=(jax.ShapeDtypeStruct((F_IN, HID), F32), j...]
    unnamed x7 -> x24, local copies, waits for them, and re-layouts: 12.4 us -> 4.64 us
    pallas_call x2 -> x0, local copies, waits for them, and re-layouts: 3.47 us -> none  [local(): pl.pallas_call(kernel, out_shape=(jax.ShapeDtypeStruct((F_IN, HID), F32),...]
    reduce_min x2 -> x0, other arithmetic: 1.51 us -> none  [the longest x1 0.76 us: local(): jnp.min(jnp.where(later, index[None, :], TILES), axis=1).astype(jnp.int32)]
where the time goes in v1:
time: 91.3 us; the launch traced here: 91.1 us
  Pallas kernels  84.3 us (92%)
  local copies, waits for them, and re-layouts  4.64 us (5%)
  between operations  2.11 us (2%)
    pallas_call x1, Pallas kernels, local(): pl.pallas_call(step, out_shape=(jax.ShapeDtypeStruct((F_IN, HID), F32), j...  69.2 us
    pallas_call x1, Pallas kernels, local(): pl.pallas_call(prepare, out_shape=(jax.ShapeDtypeStruct((NODE, NODE + HAL...  12.3 us
    unnamed x24, local copies, waits for them, and re-layouts  4.64 us
    pallas_call x1, Pallas kernels, local(): pl.pallas_call(hand_over, out_shape=tuple((jax.ShapeDtypeStruct(o.shape,...  2.84 us

profile of v1, /device:TPU:1, one launch (start us, length us, event | category | flops | bytes accessed | tf_op | source)
XLA Modules:
  0.0 91.1 jit_solution(8113726717019668189)
XLA Ops:
  0.6 0.0 copy-start.11
  0.6 0.0 copy-start.10
  0.7 0.0 copy-start.7
  0.7 0.0 copy-start.6
  0.7 0.0 copy-start.9
  0.7 0.0 copy-start.8
  2.0 12.3 %prepare.1 = (bf16[2048,4096]{1,0:T(8,128)(2,1)S(1)}, bf16[2048,1024]{1,0:T(8,128)(2,1)S(1)}, bf16[2048,128]{1,0:T(8,128)(2,1)S(1)}, bf16[2048,128]{1,0:T(8,128)...) custom-call(s32[1,192]{1,0:T(1,128)} %rows_s.1, s32[1,192]{1,0:T(1,128)} %cols_s.1, ...), custom_call_target="tpu_custom_call" | custom-call | flops 1500000000 | bytes 8000000 | tf_op jit(solution)/shard_map/prepare/pallas_call | solution.py:568
  14.4 0.0 copy-done.11
  14.4 0.0 copy-done.10
  14.4 0.0 copy-done.7
  14.4 0.0 copy-done.6
  14.4 0.0 copy-done.9
  14.4 0.0 copy-done.8
  14.4 69.2 %train_step.1 = (f32[128,256]{1,0:T(8,128)S(1)}, f32[128,256]{1,0:T(8,128)S(1)}, f32[172,256]{1,0:T(8,128)S(1)}, f32[172,256]{1,0:T(8,128)S(1)}, bf16[2048,256]{...) custom-call(s32[1]{0:T(128)S(6)} %copy.23.size_s.size_ref, bf16[2048,256]{1,0:T(8,128)(2,1)} %stale_hbm.1, ...), custom_call_target="tpu_custom_call" | custom-call | flops 20000000000 | bytes 8000000 | tf_op jit(solution)/shard_map/train_step/pallas_call | solution.py:600
  83.6 0.0 copy-start
  83.6 1.0 %copy-done = bf16[2048,256]{1,0:T(8,128)(2,1)} copy-done((bf16[2048,256]{1,0:T(8,128)(2,1)}, bf16[2048,256]{1,0:T(8,128)(2,1)S(1)}, u32[]{:S(2)}) %copy-start) | copy-done | bytes 1048600
  84.6 0.0 copy-start.1
  84.6 1.0 %copy-done.1 = bf16[2048,256]{1,0:T(8,128)(2,1)} copy-done((bf16[2048,256]{1,0:T(8,128)(2,1)}, bf16[2048,256]{1,0:T(8,128)(2,1)S(1)}, u32[]{:S(2)}) %copy-start.1) | copy-done | bytes 1048600
  85.6 0.0 copy-start.2
  85.6 0.7 copy-done.2
  86.3 0.0 copy-start.3
  86.3 0.7 copy-done.3
  86.9 0.0 copy-start.4
  86.9 0.7 copy-done.4
  87.6 0.0 copy-start.5
  87.6 0.6 copy-done.5
  88.2 2.8 %hand_over.1 = (f32[128,256]{1,0:T(8,128)}, f32[128,256]{1,0:T(8,128)}, f32[172,256]{1,0:T(8,128)}, f32[172,256]{1,0:T(8,128)}, bf16[2048,256]{1,0:T(8,128)(2,1)}, /*index=5*/bf16[2048,256]{1,0:T(8,128)(2,1)}) custom-call(f32[128,256]{1,0:T(8,128)} %copy-done.4, f32[128,256]{1,0:T(8,128)} %copy-done.5, f32[172,256]{1,0:T(8,128)} %copy-done.2, ...), custom_call_target="tpu_custom_call" | custom-call | tf_op jit(solution)/shard_map/hand_over/pallas_call | solution.py:654
Async XLA Ops:
  0.6 13.7 %copy-start.11 = (s32[2048]{0:T(1024)S(1)}, s32[2048]{0:T(1024)}, u32[]{:S(2)}) copy-start(s32[2048]{0:T(1024)} %param.29) | copy-start | bytes 24580
  0.6 13.7 %copy-start.10 = (s32[2048]{0:T(1024)S(1)}, s32[2048]{0:T(1024)}, u32[]{:S(2)}) copy-start(s32[2048]{0:T(1024)} %param.28) | copy-start | bytes 24580
  0.7 13.7 %copy-start.7 = (bf16[256,172]{0,1:T(8,128)(2,1)S(1)}, bf16[256,172]{0,1:T(8,128)(2,1)}, u32[]{:S(2)}) copy-start(bf16[256,172]{0,1:T(8,128)(2,1)} %param.20) | copy-start | bytes 264196
  0.7 13.7 %copy-start.6 = (bf16[256,172]{0,1:T(8,128)(2,1)S(1)}, bf16[256,172]{0,1:T(8,128)(2,1)}, u32[]{:S(2)}) copy-start(bf16[256,172]{0,1:T(8,128)(2,1)} %param.19) | copy-start | bytes 264196
  0.7 13.7 %copy-start.9 = (bf16[128,256]{1,0:T(8,128)(2,1)S(1)}, bf16[128,256]{1,0:T(8,128)(2,1)}, u32[]{:S(2)}) copy-start(bf16[128,256]{1,0:T(8,128)(2,1)} %w1n_ref.1) | copy-start | bytes 196612
  0.7 13.7 %copy-start.8 = (bf16[128,256]{1,0:T(8,128)(2,1)S(1)}, bf16[128,256]{1,0:T(8,128)(2,1)}, u32[]{:S(2)}) copy-start(bf16[128,256]{1,0:T(8,128)(2,1)} %w1s_ref.1) | copy-start | bytes 196612
  83.6 1.0 %copy-start = (bf16[2048,256]{1,0:T(8,128)(2,1)}, bf16[2048,256]{1,0:T(8,128)(2,1)S(1)}, u32[]{:S(2)}) copy-start(bf16[2048,256]{1,0:T(8,128)(2,1)S(1)} %get-tuple-element.34.refs_4_) | copy-start | bytes 3145732
  84.6 1.0 %copy-start.1 = (bf16[2048,256]{1,0:T(8,128)(2,1)}, bf16[2048,256]{1,0:T(8,128)(2,1)S(1)}, u32[]{:S(2)}) copy-start(bf16[2048,256]{1,0:T(8,128)(2,1)S(1)} %get-tuple-element.35.refs_5_) | copy-start | bytes 3145732
  85.6 0.7 copy-start.2
  86.3 0.7 copy-start.3
  86.9 0.7 copy-start.4
  87.6 0.6 copy-start.5

commit v2 on v1

--- a/solution.py
+++ b/solution.py
@@ -23,6 +23,7 @@
 CLSP = 176
 CH = 512
 NCH = 4
+BIG = 1024
 PIECE = 48
 SIDE = 16 * PIECE
 LOSS_SCALE = 1.0 / 32.0
@@ -143,15 +144,11 @@
 
     def clear(i, c):
         adj[at(i * BLK, BLK), :] = jnp.zeros((BLK, NODE + HALO), BF16)
+        for j in range(32):
+            state[i * 32 + j] = 0
         return c
 
     lax.fori_loop(0, NODE // BLK, clear, 0)
-
-    def clear_state(i, c):
-        state[i] = 0
-        return c
-
-    lax.fori_loop(0, 512, clear_state, 0, unroll=8)
     state[512] = 0
 
     def place(t, c):
@@ -165,17 +162,19 @@
             adj[where] = tbuf[t]
             state[block] = 1
 
-        @pl.when(known == 1)
+        @pl.when(known > 0)
         def _():
-            slot = state[512]
-            sums[slot] = adj[where].astype(F32) + tbuf[t].astype(F32)
-            slot_block[slot] = block
-            state[block] = slot + 2
-            state[512] = slot + 1
-
-        @pl.when(known > 1)
-        def _():
-            sums[known - 2] += tbuf[t].astype(F32)
+            @pl.when(known == 1)
+            def _():
+                slot = state[512]
+                sums[slot] = adj[where].astype(F32) + tbuf[t].astype(F32)
+                slot_block[slot] = block
+                state[block] = slot + 2
+                state[512] = slot + 1
+
+            @pl.when(known > 1)
+            def _():
+                sums[known - 2] += tbuf[t].astype(F32)
 
         return c
 
@@ -195,10 +194,10 @@
     size_ref, stale_hbm, grads_hbm,
     adj, pick, own, send1, upper_ref, recv_ref,
     w1s_ref, w1n_ref, w2s_ref, w2n_ref, labels_ref, mask_ref,
-    gs1_ref, gn1_ref, gs2_ref, gn2_ref, fh_hbm, fg_hbm,
+    gs1_hbm, gn1_hbm, gs2_hbm, gn2_hbm, fh_hbm, fg_hbm,
     both, agg_wide, halo, two, stale, grads, grad_t, acc1, acc2,
     gl_t, ga_t, gp_t, send2, agg_in, send3, w1, w2, fresh_buf,
-    contrib, pair_in, pair_sum, plane_in, z_in, result,
+    contrib, pair_in, pair_sum, plane_in, z_in, result, gs1_ref, gn1_ref, gs2_ref, gn2_ref,
     load_sem, ssem, rsem, local_sem,
 ):
     my_row = lax.axis_index("row")
@@ -256,12 +255,12 @@
     halo[piece_of(me), :] = jnp.zeros((SLOT, F_IN), BF16)
 
     def early_own(k, c):
-        cut = at(k * CH, CH)
+        cut = at(k * BIG, BIG)
         both[cut, 0:F_IN] = own[cut, :]
         acc1[cut, :] = dot(adj[cut, 0:NODE], own[...])
         return c
 
-    lax.fori_loop(0, NCH, early_own, 0)
+    lax.fori_loop(0, NODE // BIG, early_own, 0)
 
     load_stale.wait()
 
@@ -276,11 +275,11 @@
     lax.fori_loop(0, NCH, mask_stale, 0)
 
     def early_stale(k, c):
-        cut = at(k * CH, CH)
+        cut = at(k * BIG, BIG)
         acc2[cut, :] = dot(adj[cut, NODE : NODE + HALO], stale[...])
         return c
 
-    lax.fori_loop(0, NCH, early_stale, 0)
+    lax.fori_loop(0, NODE // BIG, early_stale, 0)
 
     load_grads.wait()
 
@@ -304,13 +303,13 @@
     wait_bytes(halo.at[pl.ds(0, HALO - SLOT)], rsem.at[0])
 
     def first_agg(k, c):
-        cut = at(k * CH, CH)
+        cut = at(k * BIG, BIG)
         agg = (acc1[cut, :] + dot(adj[cut, NODE : NODE + HALO], halo[...])).astype(BF16)
         both[cut, F_IN : 2 * F_IN] = agg
-        agg_wide[at((k & 1) * CH, CH), at((k >> 1) * F_IN, F_IN)] = agg
-        return c
-
-    lax.fori_loop(0, NCH, first_agg, 0)
+        agg_wide[:, at(k * F_IN, F_IN)] = agg
+        return c
+
+    lax.fori_loop(0, NODE // BIG, first_agg, 0)
 
     def send_agg(k, c):
         cut = at(k * CH, CH)
@@ -340,12 +339,12 @@
     lax.fori_loop(0, NCH, first_layer, 0)
 
     def second_agg(k, c):
-        cut = at(k * CH, CH)
+        cut = at(k * BIG, BIG)
         agg = acc2[cut, :] + dot(adj[cut, 0:NODE], two[:, 0:HID])
         two[cut, HID : 2 * HID] = agg.astype(BF16)
         return c
 
-    lax.fori_loop(0, NCH, second_agg, 0)
+    lax.fori_loop(0, NODE // BIG, second_agg, 0)
 
     gl_t[CLSP:HID, :] = jnp.zeros((HID - CLSP, NODE), BF16)
 
@@ -389,7 +388,7 @@
                     lanes = slice(half * BLK, (half + 1) * BLK)
                     send3[cut, lanes] = jnp.where(live, part[:, lanes], 0.0).astype(BF16)
 
-    def send_spread(k):
+    def send_spread(k, begin=0, end=COLS):
         def one(i, c):
             d = block_at(i & 3, k) * 8 + (my_zc ^ (i >> 2))
 
@@ -399,7 +398,7 @@
 
             return c
 
-        lax.fori_loop(0, COLS, one, 0)
+        lax.fori_loop(begin, end, one, 0)
 
     def part_copy(which, src, dst, d):
         pltpu.make_async_remote_copy(
@@ -484,41 +483,37 @@
         gp_t[:, cut] = jnp.where(node < size, grad * slope, 0.0).astype(BF16)
         return c
 
-    make_spread(0)
-    send_spread(0)
-    lax.fori_loop(0, 2, back_first, 0)
-    make_spread(1)
-    send_spread(1)
-    lax.fori_loop(2, NCH, back_first, 0)
+    for k in range(3):
+        make_spread(k)
+        send_spread(k)
+    lax.fori_loop(0, NCH, back_first, 0)
 
     g1 = dot(gp_t[...], both[...])
     contrib[0:HID, :] = g1[:, 0:F_IN].astype(BF16)
     contrib[HID : 2 * HID, :] = g1[:, F_IN : 2 * F_IN].astype(BF16)
     reduce_pair()
-    make_spread(2)
+    make_spread(3)
     reduce_plane()
-    send_spread(2)
-    make_spread(3)
+    send_spread(3)
     reduce_z()
-    send_spread(3)
+    wait_bytes(agg_in.at[pl.ds(0, HALO - SLOT)], rsem.at[1])
+
+    def fresh(k, c):
+        cut = at(k * CH, CH)
+        pre = dot(halo[cut, :], w1[0:F_IN, :]) + dot(agg_in[cut, :], w1[F_IN : 2 * F_IN, :])
+        fresh_buf[cut, :] = (pre / (1.0 + jnp.exp(-pre))).astype(BF16)
+        return c
+
+    lax.fori_loop(0, NCH, fresh, 0)
+    give_fresh = pltpu.make_async_copy(fresh_buf, fh_hbm, local_sem.at[1])
+    give_fresh.start()
+
+    return_plane()
     own_spread = pltpu.make_async_copy(
         send3.at[piece_of(me)], fg_hbm.at[piece_of(me)], local_sem.at[0]
     )
     own_spread.start()
 
-    wait_bytes(agg_in.at[pl.ds(0, HALO - SLOT)], rsem.at[1])
-
-    def fresh(k, c):
-        cut = at(k * CH, CH)
-        pre = dot(halo[cut, :], w1[0:F_IN, :]) + dot(agg_in[cut, :], w1[F_IN : 2 * F_IN, :])
-        fresh_buf[cut, :] = (pre / (1.0 + jnp.exp(-pre))).astype(BF16)
-        return c
-
-    lax.fori_loop(0, NCH, fresh, 0)
-    give_fresh = pltpu.make_async_copy(fresh_buf, fh_hbm, local_sem.at[1])
-    give_fresh.start()
-
-    return_plane()
     return_pair()
     wait_bytes(result.at[other], rsem.at[7])
 
@@ -527,6 +522,14 @@
     for b, (dst, half) in enumerate(((gs2_ref, 0), (gs2_ref, 1), (gn2_ref, 0), (gn2_ref, 1))):
         block = result[2 * HID + b * CLSP : 2 * HID + (b + 1) * CLSP, :].astype(F32)
         dst[:, half * BLK : (half + 1) * BLK] = block[0:CLS, :]
+    gives = [
+        pltpu.make_async_copy(src, dst, local_sem.at[2 + i])
+        for i, (src, dst) in enumerate(
+            ((gs1_ref, gs1_hbm), (gn1_ref, gn1_hbm), (gs2_ref, gs2_hbm), (gn2_ref, gn2_hbm))
+        )
+    ]
+    for give in gives:
+        give.start()
 
     wait_bytes(send1.at[pl.ds(0, HALO - SLOT)], ssem.at[0])
     wait_bytes(send2.at[pl.ds(0, HALO - SLOT)], ssem.at[1])
@@ -538,6 +541,8 @@
     wait_bytes(result.at[mine], ssem.at[7])
     own_spread.wait()
     give_fresh.wait()
+    for give in gives:
+        give.wait()
     wait_bytes(fg_hbm.at[pl.ds(0, HALO - SLOT)], rsem.at[2])
 
 
@@ -564,7 +569,6 @@
     smem = pl.BlockSpec(memory_space=pltpu.SMEM)
     vmem = pl.BlockSpec(memory_space=pltpu.VMEM)
     hbm = pl.BlockSpec(memory_space=pltpu.HBM)
-    anywhere = pl.BlockSpec(memory_space=pl.ANY)
     packed = pl.pallas_call(
         prepare,
         out_shape=(
@@ -600,15 +604,15 @@
     outs = pl.pallas_call(
         step,
         out_shape=(
-            jax.ShapeDtypeStruct((F_IN, HID), F32),
-            jax.ShapeDtypeStruct((F_IN, HID), F32),
-            jax.ShapeDtypeStruct((CLS, HID), F32),
-            jax.ShapeDtypeStruct((CLS, HID), F32),
-            jax.ShapeDtypeStruct((HALO, HID), BF16),
-            jax.ShapeDtypeStruct((HALO, HID), BF16),
+            pltpu.HBM((F_IN, HID), F32),
+            pltpu.HBM((F_IN, HID), F32),
+            pltpu.HBM((CLS, HID), F32),
+            pltpu.HBM((CLS, HID), F32),
+            pltpu.HBM((HALO, HID), BF16),
+            pltpu.HBM((HALO, HID), BF16),
         ),
         in_specs=[smem] + [hbm] * 2 + [vmem] * 12,
-        out_specs=(vmem,) * 4 + (anywhere,) * 2,
+        out_specs=(hbm,) * 6,
         scratch_shapes=[
             pltpu.VMEM((NODE, 2 * F_IN), BF16),
             pltpu.VMEM((HALF, 2 * F_IN), BF16),
@@ -634,13 +638,17 @@
             pltpu.VMEM((SIDE, BLK), BF16),
             pltpu.VMEM((4 * PIECE, BLK), BF16),
             pltpu.VMEM((2 * SIDE, BLK), BF16),
+            pltpu.VMEM((F_IN, HID), F32),
+            pltpu.VMEM((F_IN, HID), F32),
+            pltpu.VMEM((CLS, HID), F32),
+            pltpu.VMEM((CLS, HID), F32),
             pltpu.SemaphoreType.DMA((2,)),
             pltpu.SemaphoreType.DMA((8,)),
             pltpu.SemaphoreType.DMA((8,)),
-            pltpu.SemaphoreType.DMA((2,)),
+            pltpu.SemaphoreType.DMA((6,)),
         ],
         compiler_params=pltpu.CompilerParams(
-            collective_id=0, has_side_effects=True, vmem_limit_bytes=23 * 1024 * 1024
+            collective_id=0, has_side_effects=True, vmem_limit_bytes=25 * 1024 * 1024
         ),
         cost_estimate=pl.CostEstimate(
             flops=20_000_000_000, bytes_accessed=8_000_000, transcendentals=2_000_000
@@ -654,11 +662,11 @@
     gs1, gn1, gs2, gn2, fresh_hidden, fresh_grads = pl.pallas_call(
         hand_over,
         out_shape=tuple(jax.ShapeDtypeStruct(o.shape, o.dtype) for o in outs),
-        in_specs=[anywhere] * 6,
-        out_specs=(anywhere,) * 6,
+        in_specs=[hbm] * 6,
+        out_specs=(hbm,) * 6,
         scratch_shapes=[pltpu.VMEM(o.shape, o.dtype) for o in outs] + [pltpu.SemaphoreType.DMA((12,))],
         name="hand_over",
-    )(*(in_hbm(o) for o in outs))
+    )(*outs)
     return (gs1, gn1, gs2.T, gn2.T, fresh_hidden, fresh_grads)
 
 

time: 91.3 us -> 83.6 us (0.916)
  local copies, waits for them, and re-layouts: 4.64 us -> 0.03 us
  Pallas kernels: 84.3 us -> 81.2 us
    unnamed x24 -> x12, local copies, waits for them, and re-layouts: 4.64 us -> 0.03 us
    pallas_call x1, Pallas kernels: 69.2 us -> 67.6 us  [local(): pl.pallas_call(step, out_shape=(pltpu.HBM((F_IN, HID), F32), pltpu.HBM((F...]
    pallas_call x1, Pallas kernels: 12.3 us -> 10.8 us  [local(): pl.pallas_call(prepare, out_shape=(jax.ShapeDtypeStruct((NODE, NODE + HAL...]
where the time goes in v2:
time: 83.6 us; the launch traced here: 83.4 us
  Pallas kernels  81.2 us (97%)
  between operations  2.09 us (2%)
    pallas_call x1, Pallas kernels, local(): pl.pallas_call(step, out_shape=(pltpu.HBM((F_IN, HID), F32), pltpu.HBM((F...  67.6 us
    pallas_call x1, Pallas kernels, local(): pl.pallas_call(prepare, out_shape=(jax.ShapeDtypeStruct((NODE, NODE + HAL...  10.8 us
    pallas_call x1, Pallas kernels, local(): pl.pallas_call(hand_over, out_shape=tuple((jax.ShapeDtypeStruct(o.shape,...  2.85 us

profile of v2, /device:TPU:1, one launch (start us, length us, event | category | flops | bytes accessed | tf_op | source)
XLA Modules:
  0.0 83.4 jit_solution(8687661007876284139)
XLA Ops:
  0.6 0.0 copy-start.5
  0.6 0.0 copy-start.4
  0.7 0.0 copy-start.1
  0.7 0.0 copy-start
  0.7 0.0 copy-start.3
  0.7 0.0 copy-start.2
  2.0 10.8 %prepare.1 = (bf16[2048,4096]{1,0:T(8,128)(2,1)S(1)}, bf16[2048,1024]{1,0:T(8,128)(2,1)S(1)}, bf16[2048,128]{1,0:T(8,128)(2,1)S(1)}, bf16[2048,128]{1,0:T(8,128)...) custom-call(s32[1,192]{1,0:T(1,128)} %rows_s.1, s32[1,192]{1,0:T(1,128)} %cols_s.1, ...), custom_call_target="tpu_custom_call" | custom-call | flops 1500000000 | bytes 8000000 | tf_op jit(solution)/shard_map/prepare/pallas_call | solution.py:572
  12.8 0.0 copy-done.5
  12.9 0.0 copy-done.4
  12.9 0.0 copy-done.1
  12.9 0.0 copy-done
  12.9 0.0 copy-done.3
  12.9 0.0 copy-done.2
  12.9 67.6 %train_step.1 = (f32[128,256]{1,0:T(8,128)}, f32[128,256]{1,0:T(8,128)}, f32[172,256]{1,0:T(8,128)}, f32[172,256]{1,0:T(8,128)}, bf16[2048,256]{1,0:T(8,128)(2,1)}, /*index=5*/bf16[2048,256]{1,0:T(8,128)(2,1)}) custom-call(s32[1]{0:T(128)S(6)} %copy.23.size_s.size_ref, bf16[2048,256]{1,0:T(8,128)(2,1)} %stale_hbm.1, bf16[2048,256]{1,0:T(8,128)(2,1)} %grads_hbm.1, ...), custom_call_target="tpu_custom_call" | custom-call | flops 20000000000 | bytes 8000000 | tf_op jit(solution)/shard_map/train_step/pallas_call | solution.py:604
  80.5 2.8 %hand_over.1 = (f32[128,256]{1,0:T(8,128)}, f32[128,256]{1,0:T(8,128)}, f32[172,256]{1,0:T(8,128)}, f32[172,256]{1,0:T(8,128)}, bf16[2048,256]{1,0:T(8,128)(2,1)}, /*index=5*/bf16[2048,256]{1,0:T(8,128)(2,1)}) custom-call(f32[128,256]{1,0:T(8,128)} %get-tuple-element.30.refs_0_, f32[128,256]{1,0:T(8,128)} %get-tuple-element.31.refs_1_, ...), custom_call_target="tpu_custom_call" | custom-call | tf_op jit(solution)/shard_map/hand_over/pallas_call | solution.py:662
Async XLA Ops:
  0.6 12.2 %copy-start.5 = (s32[2048]{0:T(1024)S(1)}, s32[2048]{0:T(1024)}, u32[]{:S(2)}) copy-start(s32[2048]{0:T(1024)} %param.29) | copy-start | bytes 24580
  0.6 12.2 %copy-start.4 = (s32[2048]{0:T(1024)S(1)}, s32[2048]{0:T(1024)}, u32[]{:S(2)}) copy-start(s32[2048]{0:T(1024)} %param.28) | copy-start | bytes 24580
  0.7 12.2 %copy-start.1 = (bf16[256,172]{0,1:T(8,128)(2,1)S(1)}, bf16[256,172]{0,1:T(8,128)(2,1)}, u32[]{:S(2)}) copy-start(bf16[256,172]{0,1:T(8,128)(2,1)} %param.20) | copy-start | bytes 264196
  0.7 12.2 %copy-start = (bf16[256,172]{0,1:T(8,128)(2,1)S(1)}, bf16[256,172]{0,1:T(8,128)(2,1)}, u32[]{:S(2)}) copy-start(bf16[256,172]{0,1:T(8,128)(2,1)} %param.19) | copy-start | bytes 264196
  0.7 12.2 %copy-start.3 = (bf16[128,256]{1,0:T(8,128)(2,1)S(1)}, bf16[128,256]{1,0:T(8,128)(2,1)}, u32[]{:S(2)}) copy-start(bf16[128,256]{1,0:T(8,128)(2,1)} %w1n_ref.1) | copy-start | bytes 196612
  0.7 12.2 %copy-start.2 = (bf16[128,256]{1,0:T(8,128)(2,1)S(1)}, bf16[128,256]{1,0:T(8,128)(2,1)}, u32[]{:S(2)}) copy-start(bf16[128,256]{1,0:T(8,128)(2,1)} %w1s_ref.1) | copy-start | bytes 196612

commit v3 on v2

--- a/solution.py
+++ b/solution.py
@@ -63,7 +63,7 @@
 
 def prepare(
     rows_s, cols_s, count_s, size_s, tiles_hbm, feat_hbm, rows_hbm, count_hbm,
-    adj, pick, own, send1, upper_ref, recv_ref,
+    adj, pick, own, send1, upper_ref, in_count,
     tbuf, sums, own_wide, rows_ref, count_ref, state, slot_block, tile_sem, load_sem,
 ):
     me = lax.axis_index("row") * COLS + lax.axis_index("col")
@@ -90,7 +90,7 @@
     part = lax.broadcasted_iota(jnp.int32, (PARTS, BLK), 0)
     is_me = jnp.where(part == me, 1.0, 0.0).astype(BF16)
     counts = count_ref[...].astype(F32)
-    in_count = dot(counts.astype(BF16), is_me).astype(BF16)
+    in_count[...] = dot(counts.astype(BF16), is_me).astype(BF16)
     out_count = dot(jnp.transpose(counts).astype(BF16), is_me).astype(BF16)
     rows = rows_ref[...]
     high = (rows >> 7).astype(F32).astype(BF16)
@@ -115,8 +115,6 @@
         key = jnp.where(live & (low_b == q.astype(F32)), key, -1.0)
         for b in range(HALF // BLK):
             pick[cut, b * BLK : (b + 1) * BLK] = jnp.where(key == float(b), 1.0, 0.0).astype(BF16)
-        natural = jnp.where((h >> 4) == q, 1.0, 0.0).astype(BF16)
-        recv_ref[cut, :] = jnp.where(j_of < dot(natural, in_count), 1.0, 0.0).astype(BF16)
         return c
 
     lax.fori_loop(0, NCH, build_pick, 0)
@@ -180,7 +178,34 @@
 
     for k in range(TILES // STAGE):
         load_tiles(k).wait()
-        lax.fori_loop(k * STAGE, jnp.clip(used, k * STAGE, (k + 1) * STAGE), place, 0)
+        start = k * STAGE
+        here = jnp.clip(used - start, 0, STAGE)
+
+        def place_two(i, c, start=start):
+            t = start + 2 * i
+            r0, c0, r1, c1 = rows_s[0, t], cols_s[0, t], rows_s[0, t + 1], cols_s[0, t + 1]
+            first, second = r0 * 32 + c0, r1 * 32 + c1
+            fresh = (state[first] == 0) & (state[second] == 0) & (first != second)
+
+            @pl.when(fresh)
+            def _():
+                adj[at(r0 * BLK, BLK), at(c0 * BLK, BLK)] = tbuf[t]
+                adj[at(r1 * BLK, BLK), at(c1 * BLK, BLK)] = tbuf[t + 1]
+                state[first] = 1
+                state[second] = 1
+
+            @pl.when(jnp.logical_not(fresh))
+            def _():
+                place(t, 0)
+                place(t + 1, 0)
+
+            return c
+
+        lax.fori_loop(0, here >> 1, place_two, 0)
+
+        @pl.when((here & 1) == 1)
+        def _(start=start, here=here):
+            place(start + here - 1, 0)
 
     def settle(slot, c):
         block = slot_block[slot]
@@ -192,11 +217,11 @@
 
 def step(
     size_ref, stale_hbm, grads_hbm,
-    adj, pick, own, send1, upper_ref, recv_ref,
+    adj, pick, own, send1, upper_ref, in_count,
     w1s_ref, w1n_ref, w2s_ref, w2n_ref, labels_ref, mask_ref,
     gs1_hbm, gn1_hbm, gs2_hbm, gn2_hbm, fh_hbm, fg_hbm,
-    both, agg_wide, halo, two, stale, grads, grad_t, acc1, acc2,
-    gl_t, ga_t, gp_t, send2, agg_in, send3, w1, w2, fresh_buf,
+    recv_ref, both, agg_wide, halo, two, stale, grads, grad_t, acc1, acc2, acc3, w2_t, w1_t,
+    gl_t, ga_t, gp_t, send2, agg_in, send3, w1, w2,
     contrib, pair_in, pair_sum, plane_in, z_in, result, gs1_ref, gn1_ref, gs2_ref, gn2_ref,
     load_sem, ssem, rsem, local_sem,
 ):
@@ -266,6 +291,11 @@
 
     def mask_stale(k, c):
         cut = at(k * CH, CH)
+        h = lax.broadcasted_iota(jnp.int32, (CH, PARTS), 0) + k * CH
+        q = lax.broadcasted_iota(jnp.int32, (CH, PARTS), 1)
+        natural = jnp.where((h >> 4) == q, 1.0, 0.0).astype(BF16)
+        counted = dot(natural, in_count[...])
+        recv_ref[cut, :] = jnp.where((h & 15).astype(F32) < counted, 1.0, 0.0).astype(BF16)
         live = recv_ref[cut, :].astype(F32) > 0.0
         for half in range(2):
             lanes = slice(half * BLK, (half + 1) * BLK)
@@ -299,6 +329,15 @@
         return c
 
     lax.fori_loop(0, NCH, turn_grads, 0)
+
+    def scatter(k, c):
+        acc3[:, at(k * CH, CH)] = dot(grad_t[k >> 1], pick[:, at((k & 1) * CH, CH)])
+        return c
+
+    lax.fori_loop(0, NCH, scatter, 0)
+    w2_t[:, 0:HID] = jnp.transpose(w2[:, 0:HID])
+    w2_t[:, HID : 2 * HID] = jnp.transpose(w2[:, HID : 2 * HID])
+    w1_t[...] = jnp.transpose(w1[...])
 
     wait_bytes(halo.at[pl.ds(0, HALO - SLOT)], rsem.at[0])
 
@@ -363,12 +402,9 @@
 
     lax.fori_loop(0, NCH, loss_grad, 0)
 
-    w2s = jnp.transpose(w2[:, 0:HID])
-    w2n = jnp.transpose(w2[:, HID : 2 * HID])
-
     def back_agg(k, c):
         cut = at(k * CH, CH)
-        ga_t[:, cut] = dot(w2n, gl_t[:, cut]).astype(BF16)
+        ga_t[:, cut] = dot(w2_t[:, HID : 2 * HID], gl_t[:, cut]).astype(BF16)
         return c
 
     lax.fori_loop(0, NCH, back_agg, 0)
@@ -470,13 +506,11 @@
             :, b * BLK : (b + 1) * BLK
         ].astype(BF16)
 
-    w1_t = jnp.transpose(w1[...])
-
     def back_first(k, c):
         cut = at(k * CH, CH)
-        grad = dot(ga_t[...], adj[:, cut]) + dot(grad_t[k >> 1], pick[:, at((k & 1) * CH, CH)])
-        grad = grad + dot(w2s, gl_t[:, cut])
-        pre = dot_nt(w1_t, both[cut, :])
+        grad = acc3[:, cut] + dot(ga_t[...], adj[:, cut])
+        grad = grad + dot(w2_t[:, 0:HID], gl_t[:, cut])
+        pre = dot_nt(w1_t[...], both[cut, :])
         sigma = 1.0 / (1.0 + jnp.exp(-pre))
         slope = sigma * (1.0 + pre * (1.0 - sigma))
         node = lax.broadcasted_iota(jnp.int32, (HID, CH), 1) + k * CH
@@ -501,11 +535,11 @@
     def fresh(k, c):
         cut = at(k * CH, CH)
         pre = dot(halo[cut, :], w1[0:F_IN, :]) + dot(agg_in[cut, :], w1[F_IN : 2 * F_IN, :])
-        fresh_buf[cut, :] = (pre / (1.0 + jnp.exp(-pre))).astype(BF16)
+        stale[cut, :] = (pre / (1.0 + jnp.exp(-pre))).astype(BF16)
         return c
 
     lax.fori_loop(0, NCH, fresh, 0)
-    give_fresh = pltpu.make_async_copy(fresh_buf, fh_hbm, local_sem.at[1])
+    give_fresh = pltpu.make_async_copy(stale, fh_hbm, local_sem.at[1])
     give_fresh.start()
 
     return_plane()
@@ -577,7 +611,7 @@
             jax.ShapeDtypeStruct((NODE, F_IN), BF16),
             jax.ShapeDtypeStruct((HALO, F_IN), BF16),
             jax.ShapeDtypeStruct((HALO, BLK), BF16),
-            jax.ShapeDtypeStruct((HALO, BLK), BF16),
+            jax.ShapeDtypeStruct((PARTS, BLK), BF16),
         ),
         in_specs=[smem] * 4 + [hbm] * 4,
         out_specs=(vmem,) * 6,
@@ -614,6 +648,7 @@
         in_specs=[smem] + [hbm] * 2 + [vmem] * 12,
         out_specs=(hbm,) * 6,
         scratch_shapes=[
+            pltpu.VMEM((HALO, BLK), BF16),
             pltpu.VMEM((NODE, 2 * F_IN), BF16),
             pltpu.VMEM((HALF, 2 * F_IN), BF16),
             pltpu.VMEM((HALO, F_IN), BF16),
@@ -623,6 +658,9 @@
             pltpu.VMEM((2, HID, HALO), BF16),
             pltpu.VMEM((NODE, F_IN), F32),
             pltpu.VMEM((NODE, HID), F32),
+            pltpu.VMEM((HID, NODE), F32),
+            pltpu.VMEM((HID, 2 * HID), BF16),
+            pltpu.VMEM((HID, 2 * F_IN), BF16),
             pltpu.VMEM((HID, NODE), BF16),
             pltpu.VMEM((HID, NODE), BF16),
             pltpu.VMEM((HID, NODE), BF16),
@@ -631,7 +669,6 @@
             pltpu.VMEM((HALO, HID), BF16),
             pltpu.VMEM((2 * F_IN, HID), BF16),
             pltpu.VMEM((HID, 2 * HID), BF16),
-            pltpu.VMEM((HALO, HID), BF16),
             pltpu.VMEM((2 * SIDE, BLK), BF16),
             pltpu.VMEM((SIDE, BLK), BF16),
             pltpu.VMEM((SIDE, BLK), BF16),

time: 83.6 us -> 82.5 us (0.987)
  Pallas kernels: 81.2 us -> 80.1 us
    pallas_call x1, Pallas kernels: 67.6 us -> 66.3 us  [local(): pl.pallas_call(step, out_shape=(pltpu.HBM((F_IN, HID), F32), pltpu.HBM((F...]
where the time goes in v3:
time: 82.5 us; the launch traced here: 82.2 us
  Pallas kernels  80.1 us (97%)
  between operations  2.09 us (3%)
    pallas_call x1, Pallas kernels, local(): pl.pallas_call(step, out_shape=(pltpu.HBM((F_IN, HID), F32), pltpu.HBM((F...  66.3 us
    pallas_call x1, Pallas kernels, local(): pl.pallas_call(prepare, out_shape=(jax.ShapeDtypeStruct((NODE, NODE + HAL...  10.9 us
    pallas_call x1, Pallas kernels, local(): pl.pallas_call(hand_over, out_shape=tuple((jax.ShapeDtypeStruct(o.shape,...  2.85 us

profile of v3, /device:TPU:1, one launch (start us, length us, event | category | flops | bytes accessed | tf_op | source)
XLA Modules:
  0.0 82.2 jit_solution(8296395717582646963)
XLA Ops:
  0.6 0.0 copy-start.5
  0.6 0.0 copy-start.4
  0.7 0.0 copy-start.1
  0.7 0.0 copy-start
  0.7 0.0 copy-start.3
  0.7 0.0 copy-start.2
  2.0 10.9 %prepare.1 = (bf16[2048,4096]{1,0:T(8,128)(2,1)S(1)}, bf16[2048,1024]{1,0:T(8,128)(2,1)S(1)}, bf16[2048,128]{1,0:T(8,128)(2,1)S(1)}, bf16[2048,128]{1,0:T(8,128)...) custom-call(s32[1,192]{1,0:T(1,128)} %rows_s.1, s32[1,192]{1,0:T(1,128)} %cols_s.1, ...), custom_call_target="tpu_custom_call" | custom-call | flops 1500000000 | bytes 8000000 | tf_op jit(solution)/shard_map/prepare/pallas_call | solution.py:606
  13.0 0.0 copy-done.5
  13.0 0.0 copy-done.4
  13.0 0.0 copy-done.1
  13.0 0.0 copy-done
  13.0 0.0 copy-done.3
  13.0 0.0 copy-done.2
  13.0 66.3 %train_step.1 = (f32[128,256]{1,0:T(8,128)}, f32[128,256]{1,0:T(8,128)}, f32[172,256]{1,0:T(8,128)}, f32[172,256]{1,0:T(8,128)}, bf16[2048,256]{1,0:T(8,128)(2,1)}, /*index=5*/bf16[2048,256]{1,0:T(8,128)(2,1)}) custom-call(s32[1]{0:T(128)S(6)} %copy.23.size_s.size_ref, bf16[2048,256]{1,0:T(8,128)(2,1)} %stale_hbm.1, bf16[2048,256]{1,0:T(8,128)(2,1)} %grads_hbm.1, ...), custom_call_target="tpu_custom_call" | custom-call | flops 20000000000 | bytes 8000000 | tf_op jit(solution)/shard_map/train_step/pallas_call | solution.py:638
  79.4 2.8 %hand_over.1 = (f32[128,256]{1,0:T(8,128)}, f32[128,256]{1,0:T(8,128)}, f32[172,256]{1,0:T(8,128)}, f32[172,256]{1,0:T(8,128)}, bf16[2048,256]{1,0:T(8,128)(2,1)}, /*index=5*/bf16[2048,256]{1,0:T(8,128)(2,1)}) custom-call(f32[128,256]{1,0:T(8,128)} %get-tuple-element.30.refs_0_, f32[128,256]{1,0:T(8,128)} %get-tuple-element.31.refs_1_, ...), custom_call_target="tpu_custom_call" | custom-call | tf_op jit(solution)/shard_map/hand_over/pallas_call | solution.py:699
Async XLA Ops:
  0.6 12.3 %copy-start.5 = (s32[2048]{0:T(1024)S(1)}, s32[2048]{0:T(1024)}, u32[]{:S(2)}) copy-start(s32[2048]{0:T(1024)} %param.29) | copy-start | bytes 24580
  0.6 12.3 %copy-start.4 = (s32[2048]{0:T(1024)S(1)}, s32[2048]{0:T(1024)}, u32[]{:S(2)}) copy-start(s32[2048]{0:T(1024)} %param.28) | copy-start | bytes 24580
  0.7 12.3 %copy-start.1 = (bf16[256,172]{0,1:T(8,128)(2,1)S(1)}, bf16[256,172]{0,1:T(8,128)(2,1)}, u32[]{:S(2)}) copy-start(bf16[256,172]{0,1:T(8,128)(2,1)} %param.20) | copy-start | bytes 264196
  0.7 12.3 %copy-start = (bf16[256,172]{0,1:T(8,128)(2,1)S(1)}, bf16[256,172]{0,1:T(8,128)(2,1)}, u32[]{:S(2)}) copy-start(bf16[256,172]{0,1:T(8,128)(2,1)} %param.19) | copy-start | bytes 264196
  0.7 12.3 %copy-start.3 = (bf16[128,256]{1,0:T(8,128)(2,1)S(1)}, bf16[128,256]{1,0:T(8,128)(2,1)}, u32[]{:S(2)}) copy-start(bf16[128,256]{1,0:T(8,128)(2,1)} %w1n_ref.1) | copy-start | bytes 196612
  0.7 12.3 %copy-start.2 = (bf16[128,256]{1,0:T(8,128)(2,1)S(1)}, bf16[128,256]{1,0:T(8,128)(2,1)}, u32[]{:S(2)}) copy-start(bf16[128,256]{1,0:T(8,128)(2,1)} %w1s_ref.1) | copy-start | bytes 196612
